TPU v7x, 32 devices: a whole 2x2x4 slice. The times are simulated.
32 devices in a mesh: groups: 2 (over y), dom: 16 (over z, x, core).
Axes of the slice: x: 2, y: 2, z: 4, core: 2. Of those that a mesh axis runs over, the one named last changes fastest.
Arguments:
- features: bfloat16 [8192, 1024], P(('groups', 'dom')), parts along dimension 0, may hold values from -6 to 6
- cotangent: bfloat16 [8192, 1024], P(('groups', 'dom')), parts along dimension 0, may hold values from -6 to 6
- w_self: bfloat16 [1024, 1024], replicated, may hold values from -0.1875 to 0.1875
- w_neigh: bfloat16 [1024, 1024], replicated, may hold values from -0.1875 to 0.1875
- history: bfloat16 [16384, 1024], P(('groups', 'dom')), parts along dimension 0, may hold values from -6 to 6
- hist_scale: bfloat16 [16384], P(('groups', 'dom')), parts along dimension 0, may hold values from 0.29882812 to 3
- send_rows: int32 [32, 16, 4], P(('groups', 'dom')), parts along dimension 0, may hold values from 0 to 511
- recv_counts: int32 [32, 16], P(('groups', 'dom')), parts along dimension 0, may hold values from 1 to 4, as said below
- neighbours: int32 [8192, 16], P(('groups', 'dom')), parts along dimension 0, may hold values from 0 to 63, as said below
- tile_index: int32 [256, 2], P(('groups', 'dom')), parts along dimension 0, may hold values from 0 to 1
- tile_mask: int32 [256, 128, 128], P(('groups', 'dom')), parts along dimension 0, may hold values 0 or 1
Outputs:
- grad_x: bfloat16 [8192, 1024], P(('groups', 'dom')), parts along dimension 0
- grad_self: float32 [2048, 1024], P(('groups', 'dom')), parts along dimension 0
- grad_neigh: float32 [2048, 1024], P(('groups', 'dom')), parts along dimension 0
There are 2 independent parts, one for each index of `groups`. A program takes and returns all parts, laid end to end along the dimension named above; an argument that names none is the same for every part. Nothing has to cross between parts.
Inputs may be any that keep to these rules, and one draw needn't show every extreme that they name: `recv_counts`: each partition has an owner that fills all 4 slots for it. neighbours[i, k] = p * 4 + c names slot c of owner p for the partition of node i; references with c at or past recv_counts of that pair are not edges; the first reference of each node is an edge.
All inputs are finite; a program needn't handle non-finite values. No bound on the sum of `tile_mask` on one device may be relied on, other than what follows from the above.
Results may differ from a plain program's by a relative error of at most 0.0051.
Values may be sent and summed in bfloat16 or wider, within the bound.
A program may use at most 64 MiB of HBM per device.

v0:
```python
import jax
import jax.numpy as jnp
from jax import lax
from jax.sharding import PartitionSpec as P


def tiles_forward(inputs, tile_index, masks, block_size):
    row_total, feature_width = inputs.shape
    tile_count = masks.shape[0]
    local_sum = jnp.zeros((row_total, feature_width), jnp.float32)
    edges = jnp.zeros((row_total,), jnp.float32)
    for tile_number in range(tile_count):
        row_block = tile_index[tile_number, 0] * block_size
        col_block = tile_index[tile_number, 1] * block_size
        block = lax.dynamic_slice_in_dim(inputs, col_block, block_size, 0)
        product = jnp.dot(masks[tile_number], block, preferred_element_type=jnp.float32)
        older = lax.dynamic_slice_in_dim(local_sum, row_block, block_size, 0)
        local_sum = lax.dynamic_update_slice_in_dim(local_sum, older + product, row_block, 0)
        older_edges = lax.dynamic_slice_in_dim(edges, row_block, block_size, 0)
        edges = lax.dynamic_update_slice_in_dim(
            edges,
            older_edges + jnp.sum(masks[tile_number].astype(jnp.float32), axis=1),
            row_block,
            0,
        )
    return (local_sum, edges)


def tiles_backward(grad_rows, back_agg, tile_index, masks, block_size):
    tile_count = masks.shape[0]
    contract_rows = (((0,), (0,)), ((), ()))
    for tile_number in range(tile_count):
        row_block = tile_index[tile_number, 0] * block_size
        col_block = tile_index[tile_number, 1] * block_size
        block = lax.dynamic_slice_in_dim(back_agg, row_block, block_size, 0)
        product = lax.dot_general(
            masks[tile_number], block, contract_rows, preferred_element_type=jnp.float32
        )
        older = lax.dynamic_slice_in_dim(grad_rows, col_block, block_size, 0)
        grad_rows = lax.dynamic_update_slice_in_dim(grad_rows, older + product, col_block, 0)
    return grad_rows


def shards(
    features,
    cotangent,
    w_self,
    w_neigh,
    history,
    hist_scale,
    send_rows,
    recv_counts,
    neighbours,
    tile_index,
    tile_mask,
):
    row_total, feature_width = features.shape
    peer_count = lax.axis_size("dom")
    slot_cap = send_rows.shape[2]
    block_size = tile_mask.shape[1]
    picked = send_rows[0]
    out_rows = history[picked]
    out_scale = hist_scale[picked]
    got_rows, got_scale = (
        lax.all_to_all(out_rows, "dom", split_axis=0, concat_axis=0, tiled=True),
        lax.all_to_all(out_scale, "dom", split_axis=0, concat_axis=0, tiled=True),
    )
    slot_total = peer_count * slot_cap
    got_rows = got_rows.reshape(slot_total, feature_width)
    got_scale = got_scale.reshape(slot_total).astype(jnp.float32)
    masks = tile_mask.astype(jnp.bfloat16)
    local_sum, edges = tiles_forward(features, tile_index, masks, block_size)
    counts = recv_counts[0]
    owner = neighbours // slot_cap
    position = neighbours % slot_cap
    live = (position < counts[owner]).astype(jnp.float32)
    weight = live * got_scale[neighbours]
    row_ids = jnp.broadcast_to(jnp.arange(row_total, dtype=jnp.int32)[:, None], neighbours.shape)
    slot_weight = (
        jnp.zeros((row_total, slot_total), jnp.float32).at[row_ids, neighbours].add(weight)
    )
    remote_sum = jnp.dot(slot_weight, got_rows.astype(jnp.float32), precision=lax.Precision.HIGHEST)
    degree = edges + jnp.sum(live, axis=1)
    agg = ((local_sum + remote_sum) / degree[:, None]).astype(jnp.bfloat16)
    pre = jnp.dot(features, w_self, preferred_element_type=jnp.float32) + jnp.dot(
        agg, w_neigh, preferred_element_type=jnp.float32
    )
    sigma = jax.nn.sigmoid(pre)
    grad_pre = (cotangent.astype(jnp.float32) * sigma * (1.0 + pre * (1.0 - sigma))).astype(
        jnp.bfloat16
    )
    factor = float(peer_count * row_total) ** (-0.5)
    contract_rows = (((0,), (0,)), ((), ()))
    contract_cols = (((1,), (1,)), ((), ()))
    columns = features
    grad_self = lax.psum_scatter(
        lax.dot_general(columns, grad_pre, contract_rows, preferred_element_type=jnp.float32)
        * factor,
        "dom",
        scatter_dimension=0,
        tiled=True,
    )
    columns = agg
    grad_neigh = lax.psum_scatter(
        lax.dot_general(columns, grad_pre, contract_rows, preferred_element_type=jnp.float32)
        * factor,
        "dom",
        scatter_dimension=0,
        tiled=True,
    )
    back = lax.dot_general(grad_pre, w_neigh, contract_cols, preferred_element_type=jnp.float32)
    back_agg = (back / degree[:, None]).astype(jnp.bfloat16)
    grad_rows = lax.dot_general(grad_pre, w_self, contract_cols, preferred_element_type=jnp.float32)
    grad_rows = tiles_backward(grad_rows, back_agg, tile_index, masks, block_size)
    return (grad_rows.astype(jnp.bfloat16), grad_self, grad_neigh)


def solution(mesh):
    return jax.shard_map(
        shards,
        mesh=mesh,
        in_specs=(
            P(("groups", "dom"), None),
            P(("groups", "dom"), None),
            P(),
            P(),
            P(("groups", "dom"), None),
            P(("groups", "dom")),
            P(("groups", "dom"), None, None),
            P(("groups", "dom"), None),
            P(("groups", "dom"), None),
            P(("groups", "dom"), None),
            P(("groups", "dom"), None, None),
        ),
        out_specs=(
            P(("groups", "dom"), None),
            P(("groups", "dom"), None),
            P(("groups", "dom"), None),
        ),
        check_vma=False,
    )
```

profile of v0, /device:TPU:0, one launch (start us, length us, event | category | flops | bytes accessed | tf_op | source)
XLA Modules:
  0.0 274.0 jit_solution(17696518998746664092)
XLA Ops:
  7.2 0.8 compare_select_fusion.1
  8.1 0.1 reshape.119
  8.3 0.8 gather_fusion
  9.1 0.7 all_to_all.12
  9.8 7.4 %all-to-all-start = ((bf16[16,1,4]{2,1,0:T(2,128)(2,1)}), bf16[16,1,4]{2,1,0:T(2,128)(2,1)S(1)}, u32[]{:S(2)}, u32[]{:S(2)}) async-start(bf16[16,1,4]{2,1,0:T(2,128)(2,1)} %all_to_all.12), calls=%async_computation | async-start | bytes 16384 | tf_op jit(solution)/shard_map/all_to_all | solution.py:66
  17.2 0.7 fusion.73
  27.9 0.7 fusion.74
  28.9 0.1 copy.66
  29.0 0.7 reshape.141
  29.7 0.1 copy.69
  29.8 0.1 reshape.127
  29.9 0.2 convert_reduce_fusion
  30.2 1.7 fusion.75
  31.9 0.2 dynamic_update_slice.80
  32.2 1.2 fusion.33
  33.4 0.2 add_dynamic-update-slice_fusion.6
  33.6 1.2 fusion.32
  34.8 0.2 add_dynamic-update-slice_fusion.5
  35.0 1.2 fusion.30
  36.2 0.2 add_dynamic-update-slice_fusion.4
  36.4 0.3 fusion.28
  36.6 0.2 add_dynamic-update-slice_fusion.3
  36.8 0.3 fusion.26
  37.1 0.2 add_dynamic-update-slice_fusion.2
  37.2 0.3 fusion.24
  37.5 0.2 add_dynamic-update-slice_fusion.1
  37.7 0.3 fusion.22
  38.0 0.2 add_dynamic-update-slice_fusion
  38.1 0.3 fusion.20
  38.4 10.0 %convert_reduce_fusion.8 = (f32[256]{0:T(256)S(1)}, pred[256,16]{0,1:T(8,128)(4,1)S(1)}) fusion(s32[]{:T(128)} %bitcast.48, s32[]{:T(128)} %bitcast.47, s32[]{:T(128)} %bitcast.46, s32[]{:T(128)} %bitcast.45, s32[]{:T(128)} %bitcast.44, s32[]{:T(128)} %bitcast.43, s32[]{:T(128)} %bitcast.42, s32[]{:T(128)} %bitcast.41, s32[]{:T(128)} %bitcast.40, ...), kind=kLoop, calls=%fused_computation.105 | loop fusion | flops 225024 | bytes 21568 | tf_op jit(solution)/shard_map/reduce_sum | solution.py:83
  48.4 2.8 %gather_fusion.2 = bf16[64,1024]{1,0:T(8,128)(2,1)} fusion(bf16[512,1024]{1,0:T(8,128)(2,1)} %param.15, s32[1024]{0:T(1024)S(1)} %pad_clamp_fusion), kind=kCustom, calls=%fused_computation.2 | custom fusion | bytes 262400 | tf_op jit(solution)/shard_map/gather | solution.py:62
  51.2 1.6 reshape.134
  52.8 6.1 %all-to-all-start.1 = ((bf16[16,4,1024]{2,1,0:T(4,128)(2,1)}), bf16[16,4,1024]{2,1,0:T(4,128)(2,1)}, u32[]{:S(2)}, u32[]{:S(2)}) async-start(bf16[16,4,1024]{2,1,0:T(4,128)(2,1)} %reshape.134), calls=%async_computation.1 | async-start | bytes 262144 | tf_op jit(solution)/shard_map/all_to_all | solution.py:65
  59.0 24.7 %gather_fusion.1 = f32[4096]{0:T(1024)S(1)} fusion(f32[64]{0:T(128)S(1)} %reshape.93, s32[4096]{0:T(1024)S(1)} %broadcast_clamp_fusion), kind=kCustom, calls=%fused_computation.1 | custom fusion | bytes 49152 | tf_op jit(solution)/shard_map/gather | solution.py:77
  83.8 0.8 reshape.126
  84.5 1.0 copy.70
  85.5 0.6 broadcast_select_fusion.1
  86.1 0.8 copy.71
  86.9 0.7 reshape.143
  87.6 22.1 %scatter_custom_fusion = f32[16384]{0:T(1024)S(1)} fusion(s32[4096]{0:T(1024)} %reshape.141, f32[4096]{0:T(1024)} %reshape.143, f32[]{:T(128)} %constant.56.clone.1), kind=kCustom, calls=%fused_computation.94 | custom fusion | flops 4096 | bytes 66048
  109.7 0.6 reshape.91
  110.3 0.9 reshape.88
  111.3 1.6 fusion.1
  113.0 0.3 copy-done.12
  113.3 1.0 multiply_convert_fusion
  114.3 2.6 convolution_multiply_fusion
  117.0 0.2 reduce-scatter.7.cloned.1.call-start
  117.2 0.8 copy-done.4
  118.0 2.7 multiply_bitcast_fusion
  120.8 5.4 %copy.93 = f32[1024,1024]{1,0:T(8,128)} copy(f32[1024,1024]{0,1:T(8,128)} %multiply_bitcast_fusion) | data formatting | bytes 8388608
  126.2 0.7 fusion.76
  126.9 0.9 copy-done.13
  127.9 0.7 fusion.2
  128.6 0.3 fusion.18
  128.9 0.3 fusion.16
  129.2 0.3 fusion.14
  129.5 0.3 fusion.12
  129.7 0.3 fusion.10
  130.0 0.3 fusion.8
  130.3 0.3 fusion.6
  130.6 0.3 fusion.4
  130.9 0.9 convert_element_type.68
  131.7 59.1 %reduce-scatter.5.cloned.1.call-done = f32[64,1024]{1,0:T(8,128)} async-done(((f32[1024,1024]{1,0:T(8,128)}), f32[64,1024]{1,0:T(8,128)}) %reduce-scatter.5.cloned.1.call-update) | async-done | bytes 262160 | tf_op jit(solution)/shard_map/reduce_scatter | solution.py:104
  190.9 76.3 %reduce-scatter.7.cloned.1.call-done = f32[64,1024]{1,0:T(8,128)} async-done(((f32[1024,1024]{1,0:T(8,128)}), f32[64,1024]{1,0:T(8,128)}) %reduce-scatter.7.cloned.1.call-update) | async-done | bytes 262160
  (46 shorter events, 0.7 us)
Async XLA Ops:
  7.2 23.0 %copy-start = (bf16[1024,1024]{1,0:T(8,128)(2,1)S(1)}, bf16[1024,1024]{1,0:T(8,128)(2,1)}, u32[]{:S(2)}) copy-start(bf16[1024,1024]{1,0:T(8,128)(2,1)} %param.13) | copy-start | bytes 6291460
  7.2 1.0 copy-start.1
  8.2 8.9 %copy-start.9 = (s32[8,2]{0,1:T(2,128)S(1)}, s32[8,2]{0,1:T(2,128)}, u32[]{:S(2)}) copy-start(s32[8,2]{0,1:T(2,128)} %param.20) | copy-start | bytes 196
  8.2 19.7 %copy-start.7 = (s32[1,16]{1,0:T(1,128)S(1)}, s32[1,16]{1,0:T(1,128)}, u32[]{:S(2)}) copy-start(s32[1,16]{1,0:T(1,128)} %param.18) | copy-start | bytes 196
  8.3 20.4 %copy-start.8 = (s32[256,16]{0,1:T(8,128)S(1)}, s32[256,16]{0,1:T(8,128)}, u32[]{:S(2)}) copy-start(s32[256,16]{0,1:T(8,128)} %param.19) | copy-start | bytes 49156
  8.3 20.4 %copy-start.11 = (s32[2]{0:T(128)S(1)}, s32[2]{0:T(128)}, u32[]{:S(2)}) copy-start(s32[2]{0:T(128)} %constant.76) | copy-start | bytes 28
  8.3 20.5 %copy-start.10 = (s32[2]{0:T(128)S(1)}, s32[2]{0:T(128)}, u32[]{:S(2)}) copy-start(s32[2]{0:T(128)} %constant.73) | copy-start | bytes 28
  8.3 21.6 %copy-start.6 = (s32[8,128,128]{2,1,0:T(8,128)S(1)}, s32[8,128,128]{2,1,0:T(8,128)}, u32[]{:S(2)}) copy-start(s32[8,128,128]{2,1,0:T(8,128)} %param.21) | copy-start | bytes 1572868
  9.1 21.1 %copy-start.2 = (bf16[256,1024]{1,0:T(8,128)(2,1)S(1)}, bf16[256,1024]{1,0:T(8,128)(2,1)}, u32[]{:S(2)}) copy-start(bf16[256,1024]{1,0:T(8,128)(2,1)} %param.11) | copy-start | bytes 1572868
  9.8 43.0 %all-to-all-start = ((bf16[16,1,4]{2,1,0:T(2,128)(2,1)}), bf16[16,1,4]{2,1,0:T(2,128)(2,1)S(1)}, u32[]{:S(2)}, u32[]{:S(2)}) async-start(bf16[16,1,4]{2,1,0:T(2,128)(2,1)} %all_to_all.12), calls=%async_computation | async-start | bytes 16384 | tf_op jit(solution)/shard_map/all_to_all | solution.py:66
  32.1 4.3 %copy-start.3 = (bf16[256,1024]{1,0:T(8,128)(2,1)S(1)}, bf16[256,1024]{1,0:T(8,128)(2,1)}, u32[]{:S(2)}) copy-start(bf16[256,1024]{1,0:T(8,128)(2,1)} %param.11) | copy-start | bytes 1572868
  52.8 57.5 %all-to-all-start.1 = ((bf16[16,4,1024]{2,1,0:T(4,128)(2,1)}), bf16[16,4,1024]{2,1,0:T(4,128)(2,1)}, u32[]{:S(2)}, u32[]{:S(2)}) async-start(bf16[16,4,1024]{2,1,0:T(4,128)(2,1)} %reshape.134), calls=%async_computation.1 | async-start | bytes 262144 | tf_op jit(solution)/shard_map/all_to_all | solution.py:65
  58.9 132.0 %reduce-scatter.5.cloned.1.call-start = ((), (), s32[]{:S(2)}) async-start(), calls=%async_computation.4 | async-start | bytes 4456448 | tf_op jit(solution)/shard_map/reduce_scatter | solution.py:104
  111.3 1.7 copy-start.5
  111.3 1.9 copy-start.12
  111.3 2.0 copy-start.14
  117.0 1.0 copy-start.4
  117.0 150.2 %reduce-scatter.7.cloned.1.call-start = ((), (), s32[]{:S(2)}) async-start(), calls=%async_computation.5 | async-start | bytes 4456448
  126.2 1.7 copy-start.13
Sparse Core Ops, SparseCore 0:
  117.1 73.7 reduce-scatter.4
  195.8 71.3 reduce-scatter.6
where the time goes:
time: 275 us; the launch traced here: 274 us
  waiting for transfers between devices  135 us (49%)
  local copies, waits for them, and re-layouts  45.9 us (17%)
  other arithmetic  36 us (13%)
  between operations  24.5 us (9%)
  matrix products  18.4 us (7%)
  starting transfers between devices  13.7 us (5%)
    unnamed x3, waiting for transfers between devices  76.3 us
    reduce_scatter x1, waiting for transfers between devices, shards(): lax.psum_scatter(lax.dot_general(columns, grad_pre, contract_rows, prefer...  59.1 us
    gather x3, local copies, waits for them, and re-layouts, shards(): weight = live * got_scale[neighbours]  26.4 us
    unnamed x4, other arithmetic  22.2 us
    reduce_sum x1, other arithmetic, shards(): degree = edges + jnp.sum(live, axis=1)  9.98 us
    unnamed x34, local copies, waits for them, and re-layouts  9 us
    all_to_all x1, starting transfers between devices, shards(): lax.all_to_all(out_scale, 'dom', split_axis=0, concat_axis=0, tiled=True)  7.36 us
    all_to_all x1, starting transfers between devices, shards(): lax.all_to_all(out_rows, 'dom', split_axis=0, concat_axis=0, tiled=True)  6.06 us
  transfers between devices with their start and end apart: 4, of which 2 were waited for; matrix products, arithmetic and copies ran while one was open for 33% of the time, Pallas kernels for 0%

commit v1 on v0

--- a/solution.py
+++ b/solution.py
@@ -1,7 +1,351 @@
+import functools
+
 import jax
 import jax.numpy as jnp
 from jax import lax
+from jax.experimental import pallas as pl
+from jax.experimental.pallas import tpu as pltpu
 from jax.sharding import PartitionSpec as P
+
+MESH = pl.DeviceIdType.MESH
+F32 = jnp.float32
+BF16 = jnp.bfloat16
+PLANE = 4
+LANES = 128
+PER_PEER = 16
+
+
+def iota(shape, dim):
+    return lax.broadcasted_iota(jnp.int32, shape, dim)
+
+
+def dot(a, b):
+    return jnp.dot(a, b, preferred_element_type=F32)
+
+
+def dot_nt(a, b):
+    return lax.dot_general(a, b, (((1,), (1,)), ((), ())), preferred_element_type=F32)
+
+
+def dot_tn(a, b):
+    return lax.dot_general(a, b, (((0,), (0,)), ((), ())), preferred_element_type=F32)
+
+
+def step_kernel(
+    n, subs, factor,
+    hist_ref, scale_ref, send_ref, count_ref, nb_ref, index_ref, f_hbm, mask_hbm, ws_hbm, wn_hbm, ct_hbm,
+    gx_ref, gs_ref, gn_ref,
+    f_ref, mask_ref, ws_ref, wn_ref, ct_ref, load_sem,
+    out_rows, got_rows, rows_send, rows_recv,
+    adj, agg_ref, grad, g_out, g_in, g_send, g_recv,
+    f_out, f_in, f_send, f_recv, a_out, a_in, a_send, a_recv,
+    part, right_out, right_in, left_out, left_in, right_send, right_recv, left_send, left_recv,
+    swap_out, swap_in, swap_send, swap_recv,
+):
+    me = lax.axis_index("dom")
+    core = me % 2
+    x = (me // 2) % 2
+    z = me // PLANE
+    planes = n // PLANE
+    rows, width = f_hbm.shape
+    tiles, block, _ = mask_hbm.shape
+    refs = nb_ref.shape[1]
+    cap = send_ref.shape[2]
+    hist = hist_ref.shape[0]
+    segs = PER_PEER // cap
+    seg = width // segs
+    wide = n * PER_PEER
+    slots = n * cap
+    half = width // 2
+    sub = half // subs
+    units = 2 * subs
+    rblk = width // (2 * planes)
+
+    loads = []
+    for k, (src, dst) in enumerate(((f_hbm, f_ref), (mask_hbm, mask_ref), (ws_hbm, ws_ref), (wn_hbm, wn_ref), (ct_hbm, ct_ref))):
+        load = pltpu.make_async_copy(src, dst, load_sem.at[k])
+        load.start()
+        loads.append(load)
+
+    barrier = pltpu.get_barrier_semaphore()
+
+    def greet(k, carry):
+        pl.semaphore_signal(barrier, inc=1, device_id={"dom": (me + k) % n}, device_id_type=MESH)
+        return carry
+
+    lax.fori_loop(1, n, greet, 0)
+
+    sent = send_ref[0]
+    expand = jnp.where((iota((wide, n), 0) // PER_PEER) == iota((wide, n), 1), 1.0, 0.0).astype(BF16)
+    low = (sent % 256).astype(F32).astype(BF16)
+    high = (sent // 256).astype(F32).astype(BF16)
+    spread = dot(expand, low) + 256.0 * dot(expand, high)
+    pick = jnp.where(iota((wide, cap), 1) == iota((wide, cap), 0) % cap, spread, 0.0)
+    pick = jnp.sum(pick, axis=1, keepdims=True).astype(jnp.int32)
+    hot = jnp.where(iota((wide, hist), 1) == pick, scale_ref[...].astype(F32), 0.0)
+    seg_of = (iota((wide, hist), 0) // cap) % segs
+    packed = jnp.zeros((wide, seg), F32)
+    for j in range(segs):
+        packed += dot(jnp.where(seg_of == j, hot, 0.0).astype(BF16), hist_ref[:, j * seg:(j + 1) * seg])
+    out_rows[...] = packed.astype(BF16).reshape(n, PER_PEER, seg)
+
+    pl.semaphore_wait(barrier, n - 1)
+
+    def row_copy(k, source, target):
+        return pltpu.make_async_remote_copy(
+            src_ref=out_rows.at[target], dst_ref=got_rows.at[source],
+            send_sem=rows_send.at[k], recv_sem=rows_recv.at[k],
+            device_id={"dom": target}, device_id_type=MESH)
+
+    def send_rows(k, carry):
+        row_copy(k, me, (me + k) % n).start()
+        return carry
+
+    lax.fori_loop(1, n, send_rows, 0)
+    got_rows[pl.ds(me, 1)] = out_rows[pl.ds(me, 1)]
+
+    sibling = me + 1 - 2 * core
+    across = me + 2 - 4 * x
+    diagonal = sibling + 2 - 4 * x
+
+    def remote(src, dst, send, recv, target):
+        return pltpu.make_async_remote_copy(
+            src_ref=src, dst_ref=dst, send_sem=send, recv_sem=recv,
+            device_id={"dom": target}, device_id_type=MESH)
+
+    def factor_copies(out, into, send, recv):
+        return (
+            remote(out.at[:, 1 - x], into.at[1], send.at[1], recv.at[1], across),
+            remote(out.at[:, x], into.at[0], send.at[0], recv.at[0], sibling),
+            remote(into.at[1], into.at[2], send.at[2], recv.at[2], sibling),
+        )
+
+    loads[0].wait()
+    for j in range(planes):
+        f_out[j] = f_ref[:, j * 2 * rblk:(j + 1) * 2 * rblk].T.reshape(2, rblk, rows)
+    f_copies = factor_copies(f_out, f_in, f_send, f_recv)
+    f_copies[0].start()
+    f_copies[1].start()
+
+    loads[1].wait()
+    blocks = rows // block
+    degree = []
+    for b in range(blocks):
+        edges = jnp.zeros((block, 1), F32)
+        for e in range(blocks):
+            total = jnp.zeros((block, block), jnp.int32)
+            for t in range(tiles):
+                here = (index_ref[t, 0] == b).astype(jnp.int32) * (index_ref[t, 1] == e).astype(jnp.int32)
+                total += here * mask_ref[t]
+            total = total.astype(F32)
+            edges += jnp.sum(total, axis=1, keepdims=True)
+            adj[b * block:(b + 1) * block, e * block:(e + 1) * block] = total.astype(BF16)
+        degree.append(edges)
+    degree = jnp.concatenate(degree, axis=0)
+    filled = jnp.broadcast_to(count_ref[...], (8, n)).astype(F32).astype(BF16)
+    owner = jnp.where(iota((n, slots), 1) // cap == iota((n, slots), 0), 1.0, 0.0).astype(BF16)
+    filled = dot(filled, owner)[0:1]
+    live = jnp.where((iota((1, slots), 1) % cap).astype(F32) < filled, 1.0, 0.0)
+    count = jnp.zeros((rows, slots), F32)
+    for k in range(refs):
+        count += jnp.where(nb_ref[:, k:k + 1] == iota((rows, slots), 1), live, 0.0)
+    degree += jnp.sum(count, axis=1, keepdims=True)
+    count = count.astype(BF16)
+    ws_ready, wn_ready, ct_ready = loads[2:]
+    slot_of = (iota((slots, wide), 1) // PER_PEER) * cap + iota((slots, wide), 1) % cap
+    same = slot_of == iota((slots, wide), 0)
+    spread_seg = (iota((slots, wide), 1) // cap) % segs
+    spreads = []
+    for j in range(segs):
+        e_j = jnp.where(same & (spread_seg == j), 1.0, 0.0).astype(BF16)
+        spreads.append(dot(count, e_j).astype(BF16))
+    ws_ready.wait()
+    wn_ready.wait()
+    ct_ready.wait()
+
+    def got(k, carry):
+        row_copy(k, (me + n - k) % n, (me + k) % n).wait_recv()
+        return carry
+
+    lax.fori_loop(1, n, got, 0)
+    rows_in = got_rows[...].reshape(wide, seg)
+    for j in range(segs):
+        columns = slice(j * seg, (j + 1) * seg)
+        total = dot(adj[...], f_ref[:, columns]) + dot(spreads[j], rows_in)
+        agg_ref[:, columns] = (total / degree).astype(BF16)
+
+    f_copies[0].wait_recv()
+    f_copies[2].start()
+
+    for j in range(planes):
+        a_out[j] = agg_ref[:, j * 2 * rblk:(j + 1) * 2 * rblk].T.reshape(2, rblk, rows)
+    a_copies = factor_copies(a_out, a_in, a_send, a_recv)
+
+    def g_copies(s):
+        return (
+            remote(g_out.at[core, s], g_in.at[1, s], g_send.at[1, s], g_recv.at[1, s], across),
+            remote(g_out.at[1 - core, s], g_in.at[2, s], g_send.at[2, s], g_recv.at[2, s], diagonal),
+            remote(g_out.at[1 - core, s], g_in.at[0, s], g_send.at[0, s], g_recv.at[0, s], sibling),
+        )
+
+    for s in range(subs):
+        for h in range(2):
+            columns = slice(h * half + s * sub, h * half + (s + 1) * sub)
+            pre = dot(f_ref[...], ws_ref[:, columns]) + dot(agg_ref[...], wn_ref[:, columns])
+            sigma = jax.nn.sigmoid(pre)
+            value = (ct_ref[:, columns].astype(F32) * sigma * (1.0 + pre * (1.0 - sigma))).astype(BF16)
+            g_out[h, s] = value
+            grad[:, columns] = value
+        for copy in g_copies(s):
+            copy.start()
+        if s == 0:
+            a_copies[0].start()
+            a_copies[1].start()
+
+    back = (dot_nt(grad[...], wn_ref[...]) / degree).astype(BF16)
+    gx_ref[...] = (dot_nt(grad[...], ws_ref[...]) + dot_tn(adj[...], back)).astype(BF16)
+
+    def unit_of(m, s):
+        return 2 * s + m
+
+    last = planes - 1
+
+    def right(u, k):
+        return remote(right_out.at[u, k], right_in.at[u, k], right_send.at[u, k], right_recv.at[u, k], (me + PLANE) % n)
+
+    def left(u, k):
+        return remote(left_out.at[u, k], left_in.at[u, k], left_send.at[u, k], left_recv.at[u, k], (me + n - PLANE) % n)
+
+    def along(u, inner, first, final, copy, out, into, order, beyond):
+        for k in order:
+            @pl.when(beyond(k))
+            def _():
+                @pl.when(first)
+                def _():
+                    out[u, k] = part[u, k].astype(BF16)
+
+                @pl.when(jnp.logical_not(first))
+                def _():
+                    copy(u, k).wait_recv()
+                    out[u, k] = (part[u, k] + into[u, k].astype(F32)).astype(BF16)
+
+                copy(u, k).start()
+
+            @pl.when((z == k) & jnp.logical_not(first))
+            def _():
+                copy(u, k).wait_recv()
+                part[u, k] += into[u, k].astype(F32)
+
+    for t in range(units + last):
+        if t < units:
+            s, m = t // 2, t % 2
+            if m == 0:
+                for copy in g_copies(s):
+                    copy.wait_recv()
+            if t == 0:
+                f_copies[1].wait_recv()
+                f_copies[2].wait_recv()
+            if t == 1:
+                a_copies[0].wait_recv()
+                a_copies[2].start()
+                a_copies[1].wait_recv()
+                a_copies[2].wait_recv()
+            out, into = ((f_out, f_in), (a_out, a_in))[m]
+            total = dot(out[:, x].reshape(planes * rblk, rows), g_out[core, s])
+            for k in range(3):
+                total += dot(into[k].reshape(planes * rblk, rows), g_in[k, s])
+            part[t] = total.reshape(planes, rblk, sub)
+
+        @pl.when((t - z >= 0) & (t - z < units))
+        def _():
+            along(t - z, z, z == 0, None, right, right_out, right_in, range(last, 0, -1), lambda k: k > z)
+
+        away = t - (last - z)
+
+        @pl.when((away >= 0) & (away < units))
+        def _():
+            along(away, z, z == last, None, left, left_out, left_in, range(last), lambda k: k < z)
+
+    mine = rblk // 2
+    for u in range(units):
+        swap_out[u] = part[u, z, pl.ds(pl.multiple_of((1 - core) * mine, mine), mine)] * factor
+        remote(swap_out.at[u], swap_in.at[u], swap_send.at[u], swap_recv.at[u], sibling).start()
+    for u in range(units):
+        s, m = u // 2, u % 2
+        out = (gs_ref, gn_ref)[m]
+        out[:, pl.ds(pl.multiple_of(core * half + s * sub, LANES), sub)] = (
+            part[u, z, pl.ds(pl.multiple_of(core * mine, mine), mine)] * factor)
+    for u in range(units):
+        s, m = u // 2, u % 2
+        out = (gs_ref, gn_ref)[m]
+        remote(swap_out.at[u], swap_in.at[u], swap_send.at[u], swap_recv.at[u], sibling).wait()
+        out[:, pl.ds(pl.multiple_of((1 - core) * half + s * sub, LANES), sub)] = swap_in[u]
+
+    def left_rows(k, carry):
+        row_copy(k, me, (me + k) % n).wait_send()
+        return carry
+
+    lax.fori_loop(1, n, left_rows, 0)
+    for copy in (*f_copies, *a_copies):
+        copy.wait_send()
+    for s in range(subs):
+        for copy in g_copies(s):
+            copy.wait_send()
+    for u in range(units):
+        for k in range(planes):
+            @pl.when(k > z)
+            def _():
+                right(u, k).wait_send()
+
+            @pl.when(k < z)
+            def _():
+                left(u, k).wait_send()
+
+
+def fused(
+    subs, features, cotangent, w_self, w_neigh, history, hist_scale, send_rows, recv_counts, neighbours, tile_index, tile_mask
+):
+    n = lax.axis_size("dom")
+    rows, width = features.shape
+    planes = n // PLANE
+    cap = send_rows.shape[2]
+    seg = width * cap // PER_PEER
+    sub = width // 2 // subs
+    units = 2 * subs
+    rblk = width // (2 * planes)
+    factor = float(n * rows) ** (-0.5)
+    vmem = pl.BlockSpec(memory_space=pltpu.VMEM)
+    smem = pl.BlockSpec(memory_space=pltpu.SMEM)
+    anywhere = pl.BlockSpec(memory_space=pl.ANY)
+    dma = pltpu.SemaphoreType.DMA
+    V = pltpu.VMEM
+    line = (units, planes, rblk, sub)
+    scratch = [
+        V(features.shape, BF16), V(tile_mask.shape, jnp.int32), V(w_self.shape, BF16), V(w_neigh.shape, BF16),
+        V(cotangent.shape, BF16), dma((5,)),
+        V((n, PER_PEER, seg), BF16), V((n, PER_PEER, seg), BF16), dma((n,)), dma((n,)),
+        V((rows, rows), BF16), V((rows, width), BF16), V((rows, width), BF16),
+        V((2, subs, rows, sub), BF16), V((3, subs, rows, sub), BF16), dma((3, subs)), dma((3, subs)),
+        V((planes, 2, rblk, rows), BF16), V((3, planes, rblk, rows), BF16), dma((3,)), dma((3,)),
+        V((planes, 2, rblk, rows), BF16), V((3, planes, rblk, rows), BF16), dma((3,)), dma((3,)),
+        V(line, F32), V(line, BF16), V(line, BF16), V(line, BF16), V(line, BF16),
+        dma(line[:2]), dma(line[:2]), dma(line[:2]), dma(line[:2]),
+        V((units, rblk // 2, sub), F32), V((units, rblk // 2, sub), F32), dma((units,)), dma((units,)),
+    ]
+    return pl.pallas_call(
+        functools.partial(step_kernel, n, subs, factor),
+        out_shape=(
+            jax.ShapeDtypeStruct((rows, width), BF16),
+            jax.ShapeDtypeStruct((width // n, width), F32),
+            jax.ShapeDtypeStruct((width // n, width), F32),
+        ),
+        in_specs=[vmem, vmem, vmem, vmem, vmem, smem] + [anywhere] * 5,
+        out_specs=(vmem, vmem, vmem),
+        scratch_shapes=scratch,
+        compiler_params=pltpu.CompilerParams(
+            collective_id=0, has_side_effects=True, vmem_limit_bytes=48 * 1024 * 1024),
+    )(history, hist_scale.reshape(1, -1), send_rows, recv_counts, neighbours, tile_index,
+      features, tile_mask, w_self, w_neigh, cotangent)
 
 
 def tiles_forward(inputs, tile_index, masks, block_size):
@@ -41,7 +385,7 @@
     return grad_rows
 
 
-def shards(
+def plain_shards(
     features,
     cotangent,
     w_self,
@@ -115,9 +459,20 @@
     return (grad_rows.astype(jnp.bfloat16), grad_self, grad_neigh)
 
 
+def shards(subs, *args):
+    features, send_rows, tile_mask = args[0], args[6], args[10]
+    n = lax.axis_size("dom")
+    width = features.shape[1]
+    cap = send_rows.shape[2]
+    whole_blocks = n % PLANE == 0 and (2 * width) % (n * LANES) == 0
+    if whole_blocks and PER_PEER % cap == 0 and features.shape[0] % LANES == 0:
+        return fused(subs, *args)
+    return plain_shards(*args)
+
+
 def solution(mesh):
     return jax.shard_map(
-        shards,
+        functools.partial(shards, 2),
         mesh=mesh,
         in_specs=(
             P(("groups", "dom"), None),

time: 275 us -> 66.6 us (0.24)
  waiting for transfers between devices: 135 us -> 0 us
  Pallas kernels: 0 us -> 53.7 us
  other arithmetic: 36 us -> 0 us
  local copies, waits for them, and re-layouts: 45.9 us -> 11.8 us
  between operations: 24.5 us -> 0.65 us
  matrix products: 18.4 us -> 0 us
  starting transfers between devices: 13.7 us -> 0 us
    unnamed x3 -> x0, waiting for transfers between devices: 76.3 us -> none
    reduce_scatter x1 -> x0, waiting for transfers between devices: 59.1 us -> none  [shards(): lax.psum_scatter(lax.dot_general(columns, grad_pre, contract_rows, prefer...]
    pallas_call x0 -> x1, Pallas kernels: none -> 53.7 us  [fused(): pl.pallas_call(functools.partial(step_kernel, n, subs, factor), out_shape...]
    gather x7 -> x0, local copies, waits for them, and re-layouts: 32.4 us -> none  [the longest x3 26.4 us: shards(): weight = live * got_scale[neighbours]]
    unnamed x4 -> x0, other arithmetic: 22.2 us -> none
    dot_general x23 -> x0, matrix products: 18.4 us -> none  [the longest x2 5.36 us: shards(): lax.dot_general(columns, grad_pre, contract_rows, preferred_element_type=...]
    all_to_all x2 -> x0, starting transfers between devices: 13.4 us -> none  [the longest x1 7.36 us: shards(): lax.all_to_all(out_scale, 'dom', split_axis=0, concat_axis=0, tiled=True)]
    reduce_sum x2 -> x0, other arithmetic: 10.1 us -> none  [the longest x1 9.98 us: shards(): degree = edges + jnp.sum(live, axis=1)]
  transfers between devices with their start and end apart: 4 -> 0, of which waited for: 2 -> 0; matrix products, arithmetic and copies ran while one was open for 33% -> 0% of each run, Pallas kernels for 0% -> 0%
where the time goes in v1:
time: 66.6 us; the launch traced here: 66.1 us
  Pallas kernels  53.7 us (81%)
  local copies, waits for them, and re-layouts  11.8 us (18%)
    pallas_call x1, Pallas kernels, fused(): pl.pallas_call(functools.partial(step_kernel, n, subs, factor), out_shape...  53.7 us
    unnamed x18, local copies, waits for them, and re-layouts  11.1 us

profile of v1, /device:TPU:0, one launch (start us, length us, event | category | flops | bytes accessed | tf_op | source)
XLA Modules:
  0.0 66.1 jit_solution(16650301334330753929)
XLA Ops:
  0.6 0.7 %reshape.9.scale_ref = bf16[1,512]{1,0:T(2,128)(2,1)S(1)} reshape(bf16[512]{0:T(512)(128)(2,1)} %param.16) | data formatting | bytes 2048 | tf_op jit(solution)/shard_map/reshape | solution.py:347
  1.3 0.8 %copy.16.index_ref = s32[8,2]{1,0:T(8,128)S(1)} copy(s32[8,2]{0,1:T(2,128)} %param.20) | data formatting | bytes 128 | tf_op args[9]
  2.1 0.8 %copy.14.send_ref = s32[1,16,4]{2,1,0:T(8,128)S(1)} copy(s32[1,16,4]{1,2,0:T(4,128)} %param.17) | data formatting | bytes 512 | tf_op args[6]
  2.8 0.8 %copy.15.nb_ref = s32[256,16]{1,0:T(8,128)S(1)} copy(s32[256,16]{0,1:T(8,128)} %param.19) | data formatting | bytes 32768 | tf_op args[8]
  3.6 0.0 copy-start
  3.6 1.6 %copy-done = bf16[1024,1024]{1,0:T(8,128)(2,1)S(1)} copy-done((bf16[1024,1024]{1,0:T(8,128)(2,1)S(1)}, bf16[1024,1024]{1,0:T(8,128)(2,1)}, u32[]{:S(2)}) %copy-start) | copy-done | bytes 2097176
  5.2 0.0 copy-start.1
  5.2 1.2 %copy-done.1 = bf16[512,1024]{1,0:T(8,128)(2,1)S(1)} copy-done((bf16[512,1024]{1,0:T(8,128)(2,1)S(1)}, bf16[512,1024]{1,0:T(8,128)(2,1)}, u32[]{:S(2)}) %copy-start.1) | copy-done | bytes 1048600
  6.5 0.0 copy-start.2
  6.5 1.0 %copy-done.2 = bf16[256,1024]{1,0:T(8,128)(2,1)S(1)} copy-done((bf16[256,1024]{1,0:T(8,128)(2,1)S(1)}, bf16[256,1024]{1,0:T(8,128)(2,1)}, u32[]{:S(2)}) %copy-start.2) | copy-done | bytes 524312
  7.5 0.0 copy-start.3
  7.5 1.0 %copy-done.3 = s32[8,128,128]{2,1,0:T(8,128)S(1)} copy-done((s32[8,128,128]{2,1,0:T(8,128)S(1)}, s32[8,128,128]{2,1,0:T(8,128)}, u32[]{:S(2)}) %copy-start.3) | copy-done | bytes 524312
  8.5 0.0 copy-start.4
  8.5 1.0 %copy-done.4 = bf16[256,1024]{1,0:T(8,128)(2,1)S(1)} copy-done((bf16[256,1024]{1,0:T(8,128)(2,1)S(1)}, bf16[256,1024]{1,0:T(8,128)(2,1)}, u32[]{:S(2)}) %copy-start.4) | copy-done | bytes 524312
  9.6 0.0 copy-start.5
  9.6 0.7 copy-done.5
  10.2 53.7 %shard_map.130 = (bf16[256,1024]{1,0:T(8,128)(2,1)S(1)}, f32[64,1024]{1,0:T(8,128)S(1)}, f32[64,1024]{1,0:T(8,128)S(1)}) custom-call(bf16[512,1024]{1,0:T(8,128)(2,1)S(1)} %copy-done.1, bf16[1,512]{1,0:T(2,128)(2,1)S(1)} %reshape.9.scale_ref, s32[1,16,4]{2,1,0:T(8,128)S(1)} %copy.14.send_ref, s32[1,16]{1,0:T(1,128)S(1)} %copy-done.5, ...), custom_call_target="tpu_custom_call" | custom-call | tf_op jit(solution)/shard_map/pallas_call | solution.py:335
  63.9 0.8 %copy.20 = bf16[256,1024]{1,0:T(8,128)(2,1)} copy(bf16[256,1024]{1,0:T(8,128)(2,1)S(1)} %get-tuple-element.6) | data formatting | bytes 1048576
  64.7 0.7 %copy.21 = f32[64,1024]{1,0:T(8,128)} copy(f32[64,1024]{1,0:T(8,128)S(1)} %get-tuple-element.7) | data formatting | bytes 524288
  65.4 0.7 %copy.22 = f32[64,1024]{1,0:T(8,128)} copy(f32[64,1024]{1,0:T(8,128)S(1)} %get-tuple-element.8) | data formatting | bytes 524288
Async XLA Ops:
  3.6 1.6 %copy-start = (bf16[1024,1024]{1,0:T(8,128)(2,1)S(1)}, bf16[1024,1024]{1,0:T(8,128)(2,1)}, u32[]{:S(2)}) copy-start(bf16[1024,1024]{1,0:T(8,128)(2,1)} %ws_hbm.1) | copy-start | bytes 6291460
  5.2 1.2 %copy-start.1 = (bf16[512,1024]{1,0:T(8,128)(2,1)S(1)}, bf16[512,1024]{1,0:T(8,128)(2,1)}, u32[]{:S(2)}) copy-start(bf16[512,1024]{1,0:T(8,128)(2,1)} %hist_ref.1) | copy-start | bytes 3145732
  6.5 1.0 %copy-start.2 = (bf16[256,1024]{1,0:T(8,128)(2,1)S(1)}, bf16[256,1024]{1,0:T(8,128)(2,1)}, u32[]{:S(2)}) copy-start(bf16[256,1024]{1,0:T(8,128)(2,1)} %f_hbm.1) | copy-start | bytes 1572868
  7.5 1.0 %copy-start.3 = (s32[8,128,128]{2,1,0:T(8,128)S(1)}, s32[8,128,128]{2,1,0:T(8,128)}, u32[]{:S(2)}) copy-start(s32[8,128,128]{2,1,0:T(8,128)} %mask_hbm.1) | copy-start | bytes 1572868
  8.5 1.0 %copy-start.4 = (bf16[256,1024]{1,0:T(8,128)(2,1)S(1)}, bf16[256,1024]{1,0:T(8,128)(2,1)}, u32[]{:S(2)}) copy-start(bf16[256,1024]{1,0:T(8,128)(2,1)} %ct_hbm.1) | copy-start | bytes 1572868
  9.6 0.7 copy-start.5

commit v2 on v1

--- a/solution.py
+++ b/solution.py
@@ -32,10 +32,10 @@
 
 
 def step_kernel(
-    n, subs, factor,
-    hist_ref, scale_ref, send_ref, count_ref, nb_ref, index_ref, f_hbm, mask_hbm, ws_hbm, wn_hbm, ct_hbm,
+    n, subs, ahead, factor,
+    index_ref, hist_hbm, scale_hbm, send_hbm, count_hbm, nb_hbm, f_hbm, mask_hbm, ws_hbm, wn_hbm, ct_hbm,
     gx_ref, gs_ref, gn_ref,
-    f_ref, mask_ref, ws_ref, wn_ref, ct_ref, load_sem,
+    hist_ref, scale_ref, send_ref, count_ref, nb_ref, f_ref, mask_ref, ws_ref, wn_ref, ct_ref, load_sem,
     out_rows, got_rows, rows_send, rows_recv,
     adj, agg_ref, grad, g_out, g_in, g_send, g_recv,
     f_out, f_in, f_send, f_recv, a_out, a_in, a_send, a_recv,
@@ -49,8 +49,8 @@
     planes = n // PLANE
     rows, width = f_hbm.shape
     tiles, block, _ = mask_hbm.shape
-    refs = nb_ref.shape[1]
-    cap = send_ref.shape[2]
+    refs = nb_ref.shape[0]
+    cap = send_ref.shape[1]
     hist = hist_ref.shape[0]
     segs = PER_PEER // cap
     seg = width // segs
@@ -62,10 +62,11 @@
     rblk = width // (2 * planes)
 
     loads = []
-    for k, (src, dst) in enumerate(((f_hbm, f_ref), (mask_hbm, mask_ref), (ws_hbm, ws_ref), (wn_hbm, wn_ref), (ct_hbm, ct_ref))):
+    for k, (src, dst) in enumerate(((hist_hbm, hist_ref), (scale_hbm, scale_ref), (send_hbm, send_ref), (count_hbm, count_ref), (nb_hbm, nb_ref), (f_hbm, f_ref), (mask_hbm, mask_ref), (ws_hbm, ws_ref), (wn_hbm, wn_ref), (ct_hbm, ct_ref))):
         load = pltpu.make_async_copy(src, dst, load_sem.at[k])
+        loads.append(load)
+    for load in loads[:6]:
         load.start()
-        loads.append(load)
 
     barrier = pltpu.get_barrier_semaphore()
 
@@ -74,19 +75,24 @@
         return carry
 
     lax.fori_loop(1, n, greet, 0)
+
+    for load in loads[:5]:
+        load.wait()
+    for load in loads[6:]:
+        load.start()
 
     sent = send_ref[0]
     expand = jnp.where((iota((wide, n), 0) // PER_PEER) == iota((wide, n), 1), 1.0, 0.0).astype(BF16)
     low = (sent % 256).astype(F32).astype(BF16)
     high = (sent // 256).astype(F32).astype(BF16)
-    spread = dot(expand, low) + 256.0 * dot(expand, high)
+    spread = dot_nt(expand, low) + 256.0 * dot_nt(expand, high)
     pick = jnp.where(iota((wide, cap), 1) == iota((wide, cap), 0) % cap, spread, 0.0)
     pick = jnp.sum(pick, axis=1, keepdims=True).astype(jnp.int32)
-    hot = jnp.where(iota((wide, hist), 1) == pick, scale_ref[...].astype(F32), 0.0)
-    seg_of = (iota((wide, hist), 0) // cap) % segs
+    hot = jnp.where(iota((wide, hist), 1) == pick, scale_ref[...].astype(F32).reshape(1, hist), 0.0).astype(BF16)
+    seg_of = (iota((wide, 1), 0) // cap) % segs
     packed = jnp.zeros((wide, seg), F32)
     for j in range(segs):
-        packed += dot(jnp.where(seg_of == j, hot, 0.0).astype(BF16), hist_ref[:, j * seg:(j + 1) * seg])
+        packed += dot(hot * (seg_of == j).astype(BF16), hist_ref[:, j * seg:(j + 1) * seg])
     out_rows[...] = packed.astype(BF16).reshape(n, PER_PEER, seg)
 
     pl.semaphore_wait(barrier, n - 1)
@@ -120,14 +126,14 @@
             remote(into.at[1], into.at[2], send.at[2], recv.at[2], sibling),
         )
 
-    loads[0].wait()
+    loads[5].wait()
     for j in range(planes):
         f_out[j] = f_ref[:, j * 2 * rblk:(j + 1) * 2 * rblk].T.reshape(2, rblk, rows)
     f_copies = factor_copies(f_out, f_in, f_send, f_recv)
     f_copies[0].start()
     f_copies[1].start()
 
-    loads[1].wait()
+    loads[6].wait()
     blocks = rows // block
     degree = []
     for b in range(blocks):
@@ -135,7 +141,7 @@
         for e in range(blocks):
             total = jnp.zeros((block, block), jnp.int32)
             for t in range(tiles):
-                here = (index_ref[t, 0] == b).astype(jnp.int32) * (index_ref[t, 1] == e).astype(jnp.int32)
+                here = (index_ref[0, t] == b).astype(jnp.int32) * (index_ref[1, t] == e).astype(jnp.int32)
                 total += here * mask_ref[t]
             total = total.astype(F32)
             edges += jnp.sum(total, axis=1, keepdims=True)
@@ -143,22 +149,22 @@
         degree.append(edges)
     degree = jnp.concatenate(degree, axis=0)
     filled = jnp.broadcast_to(count_ref[...], (8, n)).astype(F32).astype(BF16)
-    owner = jnp.where(iota((n, slots), 1) // cap == iota((n, slots), 0), 1.0, 0.0).astype(BF16)
-    filled = dot(filled, owner)[0:1]
-    live = jnp.where((iota((1, slots), 1) % cap).astype(F32) < filled, 1.0, 0.0)
-    count = jnp.zeros((rows, slots), F32)
+    owner = jnp.where(iota((slots, n), 0) // cap == iota((slots, n), 1), 1.0, 0.0).astype(BF16)
+    filled = dot_nt(owner, filled)[:, 0:1]
+    live = jnp.where((iota((slots, 1), 0) % cap).astype(F32) < filled, 1.0, 0.0)
+    count = jnp.zeros((slots, rows), F32)
     for k in range(refs):
-        count += jnp.where(nb_ref[:, k:k + 1] == iota((rows, slots), 1), live, 0.0)
-    degree += jnp.sum(count, axis=1, keepdims=True)
+        count += jnp.where(nb_ref[k:k + 1, :] == iota((slots, rows), 0), live, 0.0)
     count = count.astype(BF16)
-    ws_ready, wn_ready, ct_ready = loads[2:]
+    degree += dot_tn(count, jnp.ones((slots, LANES), BF16))[:, 0:1]
+    ws_ready, wn_ready, ct_ready = loads[7:]
     slot_of = (iota((slots, wide), 1) // PER_PEER) * cap + iota((slots, wide), 1) % cap
     same = slot_of == iota((slots, wide), 0)
     spread_seg = (iota((slots, wide), 1) // cap) % segs
     spreads = []
     for j in range(segs):
         e_j = jnp.where(same & (spread_seg == j), 1.0, 0.0).astype(BF16)
-        spreads.append(dot(count, e_j).astype(BF16))
+        spreads.append(dot_tn(count, e_j).astype(BF16))
     ws_ready.wait()
     wn_ready.wait()
     ct_ready.wait()
@@ -196,18 +202,13 @@
             value = (ct_ref[:, columns].astype(F32) * sigma * (1.0 + pre * (1.0 - sigma))).astype(BF16)
             g_out[h, s] = value
             grad[:, columns] = value
-        for copy in g_copies(s):
-            copy.start()
-        if s == 0:
-            a_copies[0].start()
-            a_copies[1].start()
+        if s < ahead:
+            for copy in g_copies(s):
+                copy.start()
 
     back = (dot_nt(grad[...], wn_ref[...]) / degree).astype(BF16)
     gx_ref[...] = (dot_nt(grad[...], ws_ref[...]) + dot_tn(adj[...], back)).astype(BF16)
 
-    def unit_of(m, s):
-        return 2 * s + m
-
     last = planes - 1
 
     def right(u, k):
@@ -216,7 +217,7 @@
     def left(u, k):
         return remote(left_out.at[u, k], left_in.at[u, k], left_send.at[u, k], left_recv.at[u, k], (me + n - PLANE) % n)
 
-    def along(u, inner, first, final, copy, out, into, order, beyond):
+    def along(u, first, copy, out, into, order, beyond):
         for k in order:
             @pl.when(beyond(k))
             def _():
@@ -238,14 +239,20 @@
 
     for t in range(units + last):
         if t < units:
-            s, m = t // 2, t % 2
+            s, m = t % subs, t // subs
             if m == 0:
                 for copy in g_copies(s):
                     copy.wait_recv()
+                if s + ahead < subs:
+                    for copy in g_copies(s + ahead):
+                        copy.start()
+                elif s + ahead == subs:
+                    a_copies[0].start()
+                    a_copies[1].start()
             if t == 0:
                 f_copies[1].wait_recv()
                 f_copies[2].wait_recv()
-            if t == 1:
+            if t == subs:
                 a_copies[0].wait_recv()
                 a_copies[2].start()
                 a_copies[1].wait_recv()
@@ -258,25 +265,25 @@
 
         @pl.when((t - z >= 0) & (t - z < units))
         def _():
-            along(t - z, z, z == 0, None, right, right_out, right_in, range(last, 0, -1), lambda k: k > z)
+            along(t - z, z == 0, right, right_out, right_in, range(last, 0, -1), lambda k: k > z)
 
         away = t - (last - z)
 
         @pl.when((away >= 0) & (away < units))
         def _():
-            along(away, z, z == last, None, left, left_out, left_in, range(last), lambda k: k < z)
+            along(away, z == last, left, left_out, left_in, range(last), lambda k: k < z)
 
     mine = rblk // 2
     for u in range(units):
         swap_out[u] = part[u, z, pl.ds(pl.multiple_of((1 - core) * mine, mine), mine)] * factor
         remote(swap_out.at[u], swap_in.at[u], swap_send.at[u], swap_recv.at[u], sibling).start()
     for u in range(units):
-        s, m = u // 2, u % 2
+        s, m = u % subs, u // subs
         out = (gs_ref, gn_ref)[m]
         out[:, pl.ds(pl.multiple_of(core * half + s * sub, LANES), sub)] = (
             part[u, z, pl.ds(pl.multiple_of(core * mine, mine), mine)] * factor)
     for u in range(units):
-        s, m = u // 2, u % 2
+        s, m = u % subs, u // subs
         out = (gs_ref, gn_ref)[m]
         remote(swap_out.at[u], swap_in.at[u], swap_send.at[u], swap_recv.at[u], sibling).wait()
         out[:, pl.ds(pl.multiple_of((1 - core) * half + s * sub, LANES), sub)] = swap_in[u]
@@ -303,7 +310,7 @@
 
 
 def fused(
-    subs, features, cotangent, w_self, w_neigh, history, hist_scale, send_rows, recv_counts, neighbours, tile_index, tile_mask
+    subs, ahead, features, cotangent, w_self, w_neigh, history, hist_scale, send_rows, recv_counts, neighbours, tile_index, tile_mask
 ):
     n = lax.axis_size("dom")
     rows, width = features.shape
@@ -316,13 +323,15 @@
     factor = float(n * rows) ** (-0.5)
     vmem = pl.BlockSpec(memory_space=pltpu.VMEM)
     smem = pl.BlockSpec(memory_space=pltpu.SMEM)
-    anywhere = pl.BlockSpec(memory_space=pl.ANY)
+    far = pl.BlockSpec(memory_space=pltpu.HBM)
     dma = pltpu.SemaphoreType.DMA
     V = pltpu.VMEM
     line = (units, planes, rblk, sub)
     scratch = [
+        V(history.shape, BF16), V(hist_scale.shape, BF16), V((1, cap, n), jnp.int32), V(recv_counts.shape, jnp.int32),
+        V(neighbours.shape[::-1], jnp.int32),
         V(features.shape, BF16), V(tile_mask.shape, jnp.int32), V(w_self.shape, BF16), V(w_neigh.shape, BF16),
-        V(cotangent.shape, BF16), dma((5,)),
+        V(cotangent.shape, BF16), dma((10,)),
         V((n, PER_PEER, seg), BF16), V((n, PER_PEER, seg), BF16), dma((n,)), dma((n,)),
         V((rows, rows), BF16), V((rows, width), BF16), V((rows, width), BF16),
         V((2, subs, rows, sub), BF16), V((3, subs, rows, sub), BF16), dma((3, subs)), dma((3, subs)),
@@ -333,19 +342,19 @@
         V((units, rblk // 2, sub), F32), V((units, rblk // 2, sub), F32), dma((units,)), dma((units,)),
     ]
     return pl.pallas_call(
-        functools.partial(step_kernel, n, subs, factor),
+        functools.partial(step_kernel, n, subs, ahead, factor),
         out_shape=(
             jax.ShapeDtypeStruct((rows, width), BF16),
             jax.ShapeDtypeStruct((width // n, width), F32),
             jax.ShapeDtypeStruct((width // n, width), F32),
         ),
-        in_specs=[vmem, vmem, vmem, vmem, vmem, smem] + [anywhere] * 5,
+        in_specs=[smem] + [far] * 10,
         out_specs=(vmem, vmem, vmem),
         scratch_shapes=scratch,
         compiler_params=pltpu.CompilerParams(
-            collective_id=0, has_side_effects=True, vmem_limit_bytes=48 * 1024 * 1024),
-    )(history, hist_scale.reshape(1, -1), send_rows, recv_counts, neighbours, tile_index,
-      features, tile_mask, w_self, w_neigh, cotangent)
+            collective_id=0, has_side_effects=True, vmem_limit_bytes=62 * 1024 * 1024),
+    )(tile_index.T, history, hist_scale, send_rows.transpose(0, 2, 1), recv_counts, neighbours.T, features,
+      tile_mask, w_self, w_neigh, cotangent)
 
 
 def tiles_forward(inputs, tile_index, masks, block_size):
@@ -459,20 +468,20 @@
     return (grad_rows.astype(jnp.bfloat16), grad_self, grad_neigh)
 
 
-def shards(subs, *args):
+def shards(subs, ahead, *args):
     features, send_rows, tile_mask = args[0], args[6], args[10]
     n = lax.axis_size("dom")
     width = features.shape[1]
     cap = send_rows.shape[2]
     whole_blocks = n % PLANE == 0 and (2 * width) % (n * LANES) == 0
     if whole_blocks and PER_PEER % cap == 0 and features.shape[0] % LANES == 0:
-        return fused(subs, *args)
+        return fused(subs, ahead, *args)
     return plain_shards(*args)
 
 
 def solution(mesh):
     return jax.shard_map(
-        functools.partial(shards, 2),
+        functools.partial(shards, 2, 2),
         mesh=mesh,
         in_specs=(
             P(("groups", "dom"), None),

time: 66.6 us -> 61.1 us (0.917)
  local copies, waits for them, and re-layouts: 11.8 us -> 5.21 us
  Pallas kernels: 53.7 us -> 55 us
    unnamed x18 -> x3, local copies, waits for them, and re-layouts: 11.1 us -> 5.21 us
    pallas_call x1, Pallas kernels: 53.7 us -> 55 us  [fused(): pl.pallas_call(functools.partial(step_kernel, n, subs, ahead, factor), ou...]
    reshape x1 -> x0, local copies, waits for them, and re-layouts: 0.68 us -> none  [fused(): hist_scale.reshape(1, -1)]
where the time goes in v2:
time: 61.1 us; the launch traced here: 60.8 us
  Pallas kernels  55 us (90%)
  local copies, waits for them, and re-layouts  5.21 us (9%)
  between operations  0.64 us (1%)
    pallas_call x1, Pallas kernels, fused(): pl.pallas_call(functools.partial(step_kernel, n, subs, ahead, factor), ou...  55 us
    unnamed x3, local copies, waits for them, and re-layouts  5.21 us

profile of v2, /device:TPU:0, one launch (start us, length us, event | category | flops | bytes accessed | tf_op | source)
XLA Modules:
  0.0 60.8 jit_solution(12901009213929871023)
XLA Ops:
  0.6 55.0 %shard_map.130 = (bf16[256,1024]{1,0:T(8,128)(2,1)}, f32[64,1024]{1,0:T(8,128)}, f32[64,1024]{1,0:T(8,128)}) custom-call(s32[2,8]{1,0:T(2,128)} %bitcast.5, bf16[512,1024]{1,0:T(8,128)(2,1)} %hist_hbm.1, bf16[512]{0:T(512)(128)(2,1)} %scale_hbm.1, s32[1,4,16]{2,1,0:T(4,128)} %bitcast.4, s32[1,16]{1,0:T(1,128)} %count_hbm.1, s32[16,256]{1,0:T(8,128)} %bitcast.3, ...), custom_call_target="tpu_custom_call" | custom-call | tf_op jit(solution)/shard_map/pallas_call | solution.py:344
  55.6 1.9 %copy.17 = bf16[256,1024]{1,0:T(8,128)(2,1)} copy(bf16[256,1024]{1,0:T(8,128)(2,1)} %get-tuple-element.6) | data formatting | bytes 1048576
  57.5 1.7 %copy.18 = f32[64,1024]{1,0:T(8,128)} copy(f32[64,1024]{1,0:T(8,128)} %get-tuple-element.7) | data formatting | bytes 524288
  59.1 1.7 %copy.19 = f32[64,1024]{1,0:T(8,128)} copy(f32[64,1024]{1,0:T(8,128)} %get-tuple-element.8) | data formatting | bytes 524288
